TPU v7x, 256 devices: a whole 4x4x8 slice. The times are simulated.
256 devices in a mesh: depth: 16 (over x, y), tile: 16 (over z, core).
Axes of the slice: x: 4, y: 4, z: 8, core: 2. Of those that a mesh axis runs over, the one named last changes fastest.
Arguments:
- pool: bfloat16 [16, 768, 4, 4, 4096], P('depth', 'tile'), may hold values from 0 to 1
- page_table: int32 [16, 512], P('depth'), may hold values from -1 to 767, as said below
- tf_bins: int32 [256], replicated, may hold values from 0 to 15
- palette: float32 [4, 16], replicated, may hold values from 0.05 to 1
Outputs:
- image: float32 [4, 512, 4096], P(None, 'tile', 'depth')
Inputs may be any that keep to these rules, and one draw needn't show every extreme that they name: `page_table`: row d gives, for each footprint f of slab d, the pool page (pages numbered over the devices of the tile axis in order, 48 to a device) that holds its brick, or -1 for a culled brick; the nonnegative values of a row are distinct; footprint f belongs to image tile f // 32; in a row, at most 2 footprints of one image tile have their pages on one device, and exactly 2 for some pairs of tile and device.
All inputs are finite; a program needn't handle non-finite values.
Results may differ from a plain program's by a relative error of at most 0.0003.
Values may be sent and summed in bfloat16 or wider, within the bound.
No kernel may reach another device: no remote copies, remote signals or barrier semaphores. Data moves between devices by JAX's collectives and lax.ppermute only.
A program may use at most 128 MiB of HBM per device.

v0:
```python
import jax
import jax.numpy as jnp
from jax import lax
from jax.sharding import PartitionSpec as P

CAP = 2


LIGHT_X = 0.48
LIGHT_Y = 0.6
LIGHT_Z = 0.64


def carried_in(part, axis, combine, identity):
    place = lax.axis_index(axis)
    gathered = lax.all_gather(part, axis)
    state = jnp.zeros_like(part) + jnp.asarray(identity, part.dtype)

    def one(turn, state):
        return combine(state, lax.dynamic_index_in_dim(gathered, turn, 0, False))

    return lax.fori_loop(0, place, one, state)


def from_root(block, axis, holder):
    block = jnp.where(lax.axis_index(axis) == holder, block, jnp.zeros_like(block))
    return lax.psum(block, axis)


def render_pages(bricks, colour_table, depth_count):
    bins = colour_table.shape[1]
    centres = jnp.arange(bins, dtype=jnp.float32)[:, None]

    def one_brick(single):
        values = single.astype(jnp.float32)
        cells = values.shape[1]
        pixels = values.shape[2]
        scaled = values[0].reshape(1, cells * pixels) * (bins - 1)
        hats = jnp.maximum(0.0, 1.0 - jnp.abs(scaled - centres))
        rgba = jnp.dot(colour_table, hats, precision=lax.Precision.HIGHEST).reshape(
            4, cells, pixels
        )
        normal = values[1:4] * 2.0 - 1.0
        facing = LIGHT_X * normal[0] + LIGHT_Y * normal[1] + LIGHT_Z * normal[2]
        shading = 0.5 + 0.5 * jnp.tanh(facing)
        optical = rgba[3] * (4.0 / (cells * depth_count))
        through = jnp.zeros((pixels,), jnp.float32)
        colour = jnp.zeros((3, pixels), jnp.float32)
        for cell in range(cells):
            before = through
            through = through + optical[cell]
            weights = jnp.exp(-before) - jnp.exp(-through)
            colour = colour + rgba[0:3, cell] * shading[cell][None] * weights[None]
        return jnp.concatenate([colour, jnp.exp(-through)[None]], axis=0)

    return lax.map(one_brick, bricks)


def over_operator(front_part, back_part):
    return jnp.concatenate(
        [front_part[0:3] + front_part[3:4] * back_part[0:3], front_part[3:4] * back_part[3:4]],
        axis=0,
    )


def clear_image(per_tile, pixels):
    return jnp.concatenate(
        [
            jnp.zeros((3, per_tile, pixels), jnp.float32),
            jnp.ones((1, per_tile, pixels), jnp.float32),
        ],
        axis=0,
    )


def per_device(pool, page_table, tf_bins, palette):
    tile_count = lax.axis_size("tile")
    depth_count = lax.axis_size("depth")
    tile_index = lax.axis_index("tile")
    page_count = pool.shape[1]
    foot_count = page_table.shape[1]
    per_tile = foot_count // tile_count
    pixels = pool.shape[4]
    cells = pool.shape[3]
    selector = (jnp.arange(palette.shape[1])[:, None] == tf_bins[None, :]).astype(jnp.float32)
    colour_table = jnp.dot(palette, selector, precision=lax.Precision.HIGHEST)
    page_row = page_table[0]
    foot_index = jnp.arange(foot_count)
    owner_index = foot_index // per_tile
    holder = jnp.where(page_row >= 0, page_row // page_count, -1)
    earlier_same = (
        (holder[:, None] == holder[None, :])
        & (owner_index[:, None] == owner_index[None, :])
        & (foot_index[None, :] < foot_index[:, None])
    )
    slot_rank = jnp.sum(earlier_same.astype(jnp.int32), axis=1)
    slot_index = owner_index * CAP + slot_rank
    held_here = holder == tile_index
    matches = held_here[None, :] & (slot_index[None, :] == jnp.arange(tile_count * CAP)[:, None])
    local_page = jnp.sum(jnp.where(matches, page_row[None, :] - tile_index * page_count, 0), axis=1)
    filled = jnp.any(matches, axis=1)
    page_pick = filled[:, None] & (local_page[:, None] == jnp.arange(page_count)[None, :])
    own_holder = lax.dynamic_slice_in_dim(holder, tile_index * per_tile, per_tile)
    own_rank = lax.dynamic_slice_in_dim(slot_rank, tile_index * per_tile, per_tile)
    source_slot = jnp.maximum(own_holder * CAP + own_rank, 0)
    visible = own_holder >= 0
    slot_pick = (source_slot[:, None] == jnp.arange(tile_count * CAP)[None, :]).astype(jnp.float32)
    bricks = pool[0]
    flat_pages = bricks.reshape(page_count, 4 * cells * pixels)
    picked = jnp.dot(
        page_pick.astype(jnp.bfloat16), flat_pages, preferred_element_type=jnp.float32
    ).astype(jnp.bfloat16)
    outgoing = picked.reshape(tile_count, CAP, 4, cells, pixels)
    slot_block = lax.all_to_all(outgoing, "tile", split_axis=0, concat_axis=0, tiled=True)
    shaped = slot_block.reshape(-1, 4, slot_block.shape[3], pixels)
    rendered = render_pages(shaped, colour_table, depth_count)
    arrived = rendered.reshape(slot_block.shape[0], slot_block.shape[1], 4, pixels)
    arrived_rows = arrived.reshape(tile_count * CAP, 4 * pixels)
    taken_rows = jnp.dot(slot_pick, arrived_rows, precision=lax.Precision.HIGHEST).reshape(
        per_tile, 4, pixels
    )
    taken = jnp.transpose(taken_rows, (1, 0, 2))
    slab_image = jnp.where(visible[None, :, None], taken, clear_image(per_tile, pixels))
    pixel_share = pixels // depth_count
    prefix = carried_in(slab_image, "depth", over_operator, clear_image(per_tile, pixels))
    inclusive = over_operator(prefix, slab_image)
    composite = from_root(inclusive, "depth", depth_count - 1)
    first_pixel = lax.axis_index("depth") * pixel_share
    return lax.dynamic_slice_in_dim(composite, first_pixel, pixel_share, 2)


def solution(mesh):
    in_specs = (P("depth", "tile", None, None, None), P("depth", None), P(), P())
    out_specs = P(None, "tile", "depth")
    return jax.shard_map(
        per_device, mesh=mesh, in_specs=in_specs, out_specs=out_specs, check_vma=False
    )
```

profile of v0, /device:TPU:1, one launch (start us, length us, event | category | flops | bytes accessed | tf_op | source)
XLA Modules:
  0.0 1092.4 jit_solution(10728796810615909445)
XLA Ops:
  39.1 93.2 %all-to-all-done = bf16[16,2,4,4,4096]{4,3,2,1,0:T(4,128)(2,1)} async-done(((bf16[16,2,4,4,4096]{4,3,2,1,0:T(4,128)(2,1)}), bf16[16,2,4,4,4096]{4,3,2,1,0:T(4,128)(2,1)}, u32[]{:S(2)}, u32[]{:S(2)}) %all-to-all-start) | async-done | bytes 4194336 | tf_op jit(solution)/shard_map/all_to_all | solution.py:114
  132.4 598.3 %while.24 = (s32[]{:T(128)}, f32[32,4,4096]{2,1,0:T(4,128)S(1)}, bf16[32,4,4,4096]{3,2,1,0:T(4,128)(2,1)}, f32[4,256]{1,0:T(4,128)S(1)}, s32[]{:T(128)}) while((s32[]{:T(128)}, f32[32,4,4096]{2,1,0:T(4,128)S(1)}, bf16[32,4,4,4096]{3,2,1,0:T(4,128)(2,1)}, f32[4,256]{1,0:T(4,128)S(1)}, s32[]{:T(128)}) %tuple.66), condition=%wide.region_4.5_spmd.clone, body=%wide.region_3.4_spmd.clone.sunk | while | flops 218615808 | bytes 2609229 | solution.py:56
  133.3 17.2 %fusion.81 = f32[16384,4]{0,1:T(4,128)S(1)} fusion(f32[4,256]{1,0:T(4,128)S(1)} %get-tuple-element.233, f32[16384]{0:T(1024)S(1)} %bitcast.147), kind=kOutput, calls=%fused_computation.12.clone.1 | convolution fusion | flops 218103808 | bytes 331776 | tf_op jit(solution)/shard_map/while/body/eval_jaxpr/dot_general | solution.py:40
  152.0 17.2 %fusion.81 = f32[16384,4]{0,1:T(4,128)S(1)} fusion(f32[4,256]{1,0:T(4,128)S(1)} %get-tuple-element.233, f32[16384]{0:T(1024)S(1)} %bitcast.147), kind=kOutput, calls=%fused_computation.12.clone.1 | convolution fusion | flops 218103808 | bytes 331776 | tf_op jit(solution)/shard_map/while/body/eval_jaxpr/dot_general | solution.py:40
  170.7 17.2 %fusion.81 = f32[16384,4]{0,1:T(4,128)S(1)} fusion(f32[4,256]{1,0:T(4,128)S(1)} %get-tuple-element.233, f32[16384]{0:T(1024)S(1)} %bitcast.147), kind=kOutput, calls=%fused_computation.12.clone.1 | convolution fusion | flops 218103808 | bytes 331776 | tf_op jit(solution)/shard_map/while/body/eval_jaxpr/dot_general | solution.py:40
  189.4 17.2 %fusion.81 = f32[16384,4]{0,1:T(4,128)S(1)} fusion(f32[4,256]{1,0:T(4,128)S(1)} %get-tuple-element.233, f32[16384]{0:T(1024)S(1)} %bitcast.147), kind=kOutput, calls=%fused_computation.12.clone.1 | convolution fusion | flops 218103808 | bytes 331776 | tf_op jit(solution)/shard_map/while/body/eval_jaxpr/dot_general | solution.py:40
  208.1 17.2 %fusion.81 = f32[16384,4]{0,1:T(4,128)S(1)} fusion(f32[4,256]{1,0:T(4,128)S(1)} %get-tuple-element.233, f32[16384]{0:T(1024)S(1)} %bitcast.147), kind=kOutput, calls=%fused_computation.12.clone.1 | convolution fusion | flops 218103808 | bytes 331776 | tf_op jit(solution)/shard_map/while/body/eval_jaxpr/dot_general | solution.py:40
  226.8 17.2 %fusion.81 = f32[16384,4]{0,1:T(4,128)S(1)} fusion(f32[4,256]{1,0:T(4,128)S(1)} %get-tuple-element.233, f32[16384]{0:T(1024)S(1)} %bitcast.147), kind=kOutput, calls=%fused_computation.12.clone.1 | convolution fusion | flops 218103808 | bytes 331776 | tf_op jit(solution)/shard_map/while/body/eval_jaxpr/dot_general | solution.py:40
  245.5 17.2 %fusion.81 = f32[16384,4]{0,1:T(4,128)S(1)} fusion(f32[4,256]{1,0:T(4,128)S(1)} %get-tuple-element.233, f32[16384]{0:T(1024)S(1)} %bitcast.147), kind=kOutput, calls=%fused_computation.12.clone.1 | convolution fusion | flops 218103808 | bytes 331776 | tf_op jit(solution)/shard_map/while/body/eval_jaxpr/dot_general | solution.py:40
  282.9 17.2 %fusion.81 = f32[16384,4]{0,1:T(4,128)S(1)} fusion(f32[4,256]{1,0:T(4,128)S(1)} %get-tuple-element.233, f32[16384]{0:T(1024)S(1)} %bitcast.147), kind=kOutput, calls=%fused_computation.12.clone.1 | convolution fusion | flops 218103808 | bytes 331776 | tf_op jit(solution)/shard_map/while/body/eval_jaxpr/dot_general | solution.py:40
  301.6 17.2 %fusion.81 = f32[16384,4]{0,1:T(4,128)S(1)} fusion(f32[4,256]{1,0:T(4,128)S(1)} %get-tuple-element.233, f32[16384]{0:T(1024)S(1)} %bitcast.147), kind=kOutput, calls=%fused_computation.12.clone.1 | convolution fusion | flops 218103808 | bytes 331776 | tf_op jit(solution)/shard_map/while/body/eval_jaxpr/dot_general | solution.py:40
  320.3 17.2 %fusion.81 = f32[16384,4]{0,1:T(4,128)S(1)} fusion(f32[4,256]{1,0:T(4,128)S(1)} %get-tuple-element.233, f32[16384]{0:T(1024)S(1)} %bitcast.147), kind=kOutput, calls=%fused_computation.12.clone.1 | convolution fusion | flops 218103808 | bytes 331776 | tf_op jit(solution)/shard_map/while/body/eval_jaxpr/dot_general | solution.py:40
  339.0 17.2 %fusion.81 = f32[16384,4]{0,1:T(4,128)S(1)} fusion(f32[4,256]{1,0:T(4,128)S(1)} %get-tuple-element.233, f32[16384]{0:T(1024)S(1)} %bitcast.147), kind=kOutput, calls=%fused_computation.12.clone.1 | convolution fusion | flops 218103808 | bytes 331776 | tf_op jit(solution)/shard_map/while/body/eval_jaxpr/dot_general | solution.py:40
  357.7 17.2 %fusion.81 = f32[16384,4]{0,1:T(4,128)S(1)} fusion(f32[4,256]{1,0:T(4,128)S(1)} %get-tuple-element.233, f32[16384]{0:T(1024)S(1)} %bitcast.147), kind=kOutput, calls=%fused_computation.12.clone.1 | convolution fusion | flops 218103808 | bytes 331776 | tf_op jit(solution)/shard_map/while/body/eval_jaxpr/dot_general | solution.py:40
  376.4 17.2 %fusion.81 = f32[16384,4]{0,1:T(4,128)S(1)} fusion(f32[4,256]{1,0:T(4,128)S(1)} %get-tuple-element.233, f32[16384]{0:T(1024)S(1)} %bitcast.147), kind=kOutput, calls=%fused_computation.12.clone.1 | convolution fusion | flops 218103808 | bytes 331776 | tf_op jit(solution)/shard_map/while/body/eval_jaxpr/dot_general | solution.py:40
  413.8 17.2 %fusion.81 = f32[16384,4]{0,1:T(4,128)S(1)} fusion(f32[4,256]{1,0:T(4,128)S(1)} %get-tuple-element.233, f32[16384]{0:T(1024)S(1)} %bitcast.147), kind=kOutput, calls=%fused_computation.12.clone.1 | convolution fusion | flops 218103808 | bytes 331776 | tf_op jit(solution)/shard_map/while/body/eval_jaxpr/dot_general | solution.py:40
  432.5 17.2 %fusion.81 = f32[16384,4]{0,1:T(4,128)S(1)} fusion(f32[4,256]{1,0:T(4,128)S(1)} %get-tuple-element.233, f32[16384]{0:T(1024)S(1)} %bitcast.147), kind=kOutput, calls=%fused_computation.12.clone.1 | convolution fusion | flops 218103808 | bytes 331776 | tf_op jit(solution)/shard_map/while/body/eval_jaxpr/dot_general | solution.py:40
  451.2 17.2 %fusion.81 = f32[16384,4]{0,1:T(4,128)S(1)} fusion(f32[4,256]{1,0:T(4,128)S(1)} %get-tuple-element.233, f32[16384]{0:T(1024)S(1)} %bitcast.147), kind=kOutput, calls=%fused_computation.12.clone.1 | convolution fusion | flops 218103808 | bytes 331776 | tf_op jit(solution)/shard_map/while/body/eval_jaxpr/dot_general | solution.py:40
  469.9 17.2 %fusion.81 = f32[16384,4]{0,1:T(4,128)S(1)} fusion(f32[4,256]{1,0:T(4,128)S(1)} %get-tuple-element.233, f32[16384]{0:T(1024)S(1)} %bitcast.147), kind=kOutput, calls=%fused_computation.12.clone.1 | convolution fusion | flops 218103808 | bytes 331776 | tf_op jit(solution)/shard_map/while/body/eval_jaxpr/dot_general | solution.py:40
  488.6 17.2 %fusion.81 = f32[16384,4]{0,1:T(4,128)S(1)} fusion(f32[4,256]{1,0:T(4,128)S(1)} %get-tuple-element.233, f32[16384]{0:T(1024)S(1)} %bitcast.147), kind=kOutput, calls=%fused_computation.12.clone.1 | convolution fusion | flops 218103808 | bytes 331776 | tf_op jit(solution)/shard_map/while/body/eval_jaxpr/dot_general | solution.py:40
  507.3 17.2 %fusion.81 = f32[16384,4]{0,1:T(4,128)S(1)} fusion(f32[4,256]{1,0:T(4,128)S(1)} %get-tuple-element.233, f32[16384]{0:T(1024)S(1)} %bitcast.147), kind=kOutput, calls=%fused_computation.12.clone.1 | convolution fusion | flops 218103808 | bytes 331776 | tf_op jit(solution)/shard_map/while/body/eval_jaxpr/dot_general | solution.py:40
  526.0 17.2 %fusion.81 = f32[16384,4]{0,1:T(4,128)S(1)} fusion(f32[4,256]{1,0:T(4,128)S(1)} %get-tuple-element.233, f32[16384]{0:T(1024)S(1)} %bitcast.147), kind=kOutput, calls=%fused_computation.12.clone.1 | convolution fusion | flops 218103808 | bytes 331776 | tf_op jit(solution)/shard_map/while/body/eval_jaxpr/dot_general | solution.py:40
  544.7 17.2 %fusion.81 = f32[16384,4]{0,1:T(4,128)S(1)} fusion(f32[4,256]{1,0:T(4,128)S(1)} %get-tuple-element.233, f32[16384]{0:T(1024)S(1)} %bitcast.147), kind=kOutput, calls=%fused_computation.12.clone.1 | convolution fusion | flops 218103808 | bytes 331776 | tf_op jit(solution)/shard_map/while/body/eval_jaxpr/dot_general | solution.py:40
  563.4 17.2 %fusion.81 = f32[16384,4]{0,1:T(4,128)S(1)} fusion(f32[4,256]{1,0:T(4,128)S(1)} %get-tuple-element.233, f32[16384]{0:T(1024)S(1)} %bitcast.147), kind=kOutput, calls=%fused_computation.12.clone.1 | convolution fusion | flops 218103808 | bytes 331776 | tf_op jit(solution)/shard_map/while/body/eval_jaxpr/dot_general | solution.py:40
  582.1 17.2 %fusion.81 = f32[16384,4]{0,1:T(4,128)S(1)} fusion(f32[4,256]{1,0:T(4,128)S(1)} %get-tuple-element.233, f32[16384]{0:T(1024)S(1)} %bitcast.147), kind=kOutput, calls=%fused_computation.12.clone.1 | convolution fusion | flops 218103808 | bytes 331776 | tf_op jit(solution)/shard_map/while/body/eval_jaxpr/dot_general | solution.py:40
  600.8 17.2 %fusion.81 = f32[16384,4]{0,1:T(4,128)S(1)} fusion(f32[4,256]{1,0:T(4,128)S(1)} %get-tuple-element.233, f32[16384]{0:T(1024)S(1)} %bitcast.147), kind=kOutput, calls=%fused_computation.12.clone.1 | convolution fusion | flops 218103808 | bytes 331776 | tf_op jit(solution)/shard_map/while/body/eval_jaxpr/dot_general | solution.py:40
  638.2 17.2 %fusion.81 = f32[16384,4]{0,1:T(4,128)S(1)} fusion(f32[4,256]{1,0:T(4,128)S(1)} %get-tuple-element.233, f32[16384]{0:T(1024)S(1)} %bitcast.147), kind=kOutput, calls=%fused_computation.12.clone.1 | convolution fusion | flops 218103808 | bytes 331776 | tf_op jit(solution)/shard_map/while/body/eval_jaxpr/dot_general | solution.py:40
  656.9 17.2 %fusion.81 = f32[16384,4]{0,1:T(4,128)S(1)} fusion(f32[4,256]{1,0:T(4,128)S(1)} %get-tuple-element.233, f32[16384]{0:T(1024)S(1)} %bitcast.147), kind=kOutput, calls=%fused_computation.12.clone.1 | convolution fusion | flops 218103808 | bytes 331776 | tf_op jit(solution)/shard_map/while/body/eval_jaxpr/dot_general | solution.py:40
  675.6 17.2 %fusion.81 = f32[16384,4]{0,1:T(4,128)S(1)} fusion(f32[4,256]{1,0:T(4,128)S(1)} %get-tuple-element.233, f32[16384]{0:T(1024)S(1)} %bitcast.147), kind=kOutput, calls=%fused_computation.12.clone.1 | convolution fusion | flops 218103808 | bytes 331776 | tf_op jit(solution)/shard_map/while/body/eval_jaxpr/dot_general | solution.py:40
  694.3 17.2 %fusion.81 = f32[16384,4]{0,1:T(4,128)S(1)} fusion(f32[4,256]{1,0:T(4,128)S(1)} %get-tuple-element.233, f32[16384]{0:T(1024)S(1)} %bitcast.147), kind=kOutput, calls=%fused_computation.12.clone.1 | convolution fusion | flops 218103808 | bytes 331776 | tf_op jit(solution)/shard_map/while/body/eval_jaxpr/dot_general | solution.py:40
  734.5 201.5 %all-gather.3.cloned.1.call-done = f32[64,32,4096]{2,1,0:T(8,128)} async-done(((f32[4,32,4096]{2,1,0:T(8,128)}), f32[64,32,4096]{2,1,0:T(8,128)}) %all-gather.3.cloned.1.call-update) | async-done | bytes 33554448 | tf_op jit(solution)/shard_map/all_gather | solution.py:16
  939.8 144.2 %all-reduce.3.cloned.1.call-done = f32[4,32,4096]{2,1,0:T(8,128)} async-done(((f32[4,32,4096]{2,1,0:T(8,128)}), f32[4,32,4096]{2,1,0:T(8,128)}) %all-reduce.3.cloned.1.call-update) | async-done | bytes 2097168 | tf_op jit(solution)/shard_map/psum | solution.py:27
  (394 shorter events, 156.5 us)
Async XLA Ops:
  6.5 32.5 %copy-start = (f32[4,16]{1,0:T(4,128)S(1)}, f32[4,16]{1,0:T(4,128)}, u32[]{:S(2)}) copy-start(f32[4,16]{1,0:T(4,128)} %param.11) | copy-start | bytes 772
  6.5 8.8 copy-start.3
  28.7 10.4 copy-start.4
  28.7 103.7 %all-to-all-start = ((bf16[16,2,4,4,4096]{4,3,2,1,0:T(4,128)(2,1)}), bf16[16,2,4,4,4096]{4,3,2,1,0:T(4,128)(2,1)}, u32[]{:S(2)}, u32[]{:S(2)}) async-start(bf16[16,2,4,4,4096]{4,3,2,1,0:T(4,128)(2,1)} %reshape.136), calls=%async_computation | async-start | bytes 8388608 | tf_op jit(solution)/shard_map/all_to_all | solution.py:114
  38.8 897.3 %all-gather.3.cloned.1.call-start = ((), (), s32[]{:S(2)}) async-start(), calls=%async_computation.2 | async-start | bytes 35651584 | tf_op jit(solution)/shard_map/all_gather | solution.py:16
  734.5 349.5 %all-reduce.3.cloned.1.call-start = ((), (), s32[]{:S(2)}) async-start(), calls=%async_computation.1 | async-start | bytes 4194304 | tf_op jit(solution)/shard_map/psum | solution.py:27
  936.3 1.7 copy-start.2
  938.3 147.2 %copy-start.1 = (f32[4,16]{1,0:T(4,128)S(1)}, f32[4,16]{1,0:T(4,128)}, u32[]{:S(2)}) copy-start(f32[4,16]{1,0:T(4,128)} %param.11) | copy-start | bytes 772
Sparse Core Ops, SparseCore 0:
  734.6 201.4 all-gather.2
  939.9 143.9 all-reduce.2
where the time goes:
time: 1090 us
  matrix products  559 us (51%)
  waiting for transfers between devices  439 us (40%)
  other arithmetic  48.3 us (4%)
  local copies, waits for them, and re-layouts  19.3 us (2%)
  between operations  13.5 us (1%)
    dot_general x32, matrix products, one_brick(): jnp.dot(colour_table, hats, precision=lax.Precision.HIGHEST)  549 us
    all_gather x1, waiting for transfers between devices, carried_in(): gathered = lax.all_gather(part, axis)  202 us
    psum x1, waiting for transfers between devices, from_root(): return lax.psum(block, axis)  144 us
    all_to_all x1, waiting for transfers between devices, per_device(): lax.all_to_all(outgoing, 'tile', split_axis=0, concat_axis=0, tiled=True)  93.2 us
    convert_element_type x32, other arithmetic, one_brick(): values = single.astype(jnp.float32)  29.7 us
  transfers between devices with their start and end apart: 3, of which 3 were waited for; matrix products, arithmetic and copies ran while one was open for 0% of the time, Pallas kernels for 0%

commit v1 on v0

v1 whole, which is shorter than its diff:
```python
import functools

import jax
import jax.numpy as jnp
from jax import lax
from jax.experimental import pallas as pl
from jax.experimental.pallas import tpu as pltpu
from jax.sharding import PartitionSpec as P

BINS = 256
LANES = 128
SUB = 8
CAP = 2
LIGHT_X = 0.48
LIGHT_Y = 0.6
LIGHT_Z = 0.64
LOG2E = 1.4426950408889634
FULL = 65535.0
REACH = 0.2213
AHEAD = 2
SLOTS = 4


def render_kernel(table_ref, bins_ref, palette_ref, pool_ref, out_ref, pages, cells32, wide, sems, *, tiles, per_tile, page_count):
    mine = lax.axis_index("tile")
    first_page = mine * page_count

    def find(tile):
        one = jnp.int32(-1)
        two = jnp.int32(-1)
        for foot in range(per_tile):
            local = table_ref[0, tile * per_tile + foot] - first_page
            here = (local >= 0) & (local < page_count)
            two = jnp.where(here & (one >= 0), local, two)
            one = jnp.where(here & (one < 0), local, one)
        return jnp.maximum(one, 0), jnp.maximum(two, 0)

    def fetch(slot, rank, page):
        return pltpu.make_async_copy(pool_ref.at[page], pages.at[slot, rank], sems.at[slot, rank])

    def begin(tile):
        picked = find(tile)
        for rank in range(CAP):
            fetch(lax.rem(tile, SLOTS), rank, picked[rank]).start()

    for tile in range(AHEAD):
        begin(jnp.int32(tile))

    def gather(table, index):
        return jnp.take_along_axis(table, index, axis=1, mode="promise_in_bounds")

    wide[...] = jnp.zeros_like(wide)
    wide[0:4, 0:16] = palette_ref[...]
    palette = wide[...]
    low_bins = jnp.broadcast_to(bins_ref[0:1, :], (SUB, LANES))
    high_bins = jnp.broadcast_to(bins_ref[1:2, :], (SUB, LANES))
    lane = lax.broadcasted_iota(jnp.int32, (SUB, LANES), 1)
    zero = jnp.zeros((SUB, LANES), jnp.int32)
    following = (lane + 1) & (LANES - 1)
    high_next = gather(high_bins, following)
    low_next = jnp.where(lane == LANES - 1, gather(high_bins, zero), gather(low_bins, following))

    def coded(bins):
        return (gather(palette, bins) * FULL + 0.5).astype(jnp.int32)

    low_table = coded(low_bins) | lax.shift_left(coded(low_next), 16)
    high_table = coded(high_bins) | lax.shift_left(coded(high_next), 16)
    tables = []
    for channel in range(4):
        tables.append(
            tuple(jnp.broadcast_to(t[channel : channel + 1, :], (SUB, LANES)) for t in (low_table, high_table))
        )

    def one_tile(tile, _):
        @pl.when(tile + AHEAD < tiles)
        def _():
            begin(tile + AHEAD)

        slot = lax.rem(tile, SLOTS)
        for rank in range(CAP):
            fetch(slot, rank, 0).wait()
            for field in range(4):
                cells32[rank, field] = pages[slot, rank, field].astype(jnp.float32)
            for half in range(2):
                for odd in range(2):
                    colour = [None] * 3
                    through = None
                    before = None
                    for cell in range(4):
                        rows = pl.ds(64 * half + 4 * odd + cell, SUB, stride=8)
                        scalar, normal_x, normal_y, normal_z = (cells32[rank, field, rows, :] for field in range(4))
                        scaled = scalar * (BINS - 1.0)
                        index = jnp.minimum(scaled.astype(jnp.int32), BINS - 2)
                        up = scaled - index.astype(jnp.float32)
                        upper_half = index >= LANES
                        lane_index = index & (LANES - 1)
                        rgba = []
                        for low, high in tables:
                            both = jnp.where(upper_half, gather(high, lane_index), gather(low, lane_index))
                            here = (both & 0xFFFF).astype(jnp.float32)
                            beyond = lax.shift_right_logical(both, 16).astype(jnp.float32)
                            rgba.append(here + (beyond - here) * up)
                        facing = (
                            normal_x * (2 * LIGHT_X)
                            + normal_y * (2 * LIGHT_Y)
                            + normal_z * (2 * LIGHT_Z)
                            - (LIGHT_X + LIGHT_Y + LIGHT_Z)
                        )
                        shading = 0.5 + 0.5 * jnp.tanh(facing)
                        optical = rgba[3] * (-LOG2E / (16.0 * FULL))
                        through = optical if cell == 0 else through + optical
                        after = jnp.exp2(through)
                        weight = shading * ((1.0 if cell == 0 else before) - after)
                        before = after
                        for c in range(3):
                            term = rgba[c] * weight
                            colour[c] = term if cell == 0 else colour[c] + term
                    coded_parts = []
                    for c in range(3):
                        square = colour[c] * (FULL / REACH)
                        root = square * lax.rsqrt(jnp.maximum(square, 1e-20))
                        coded_parts.append((root + 0.5).astype(jnp.int32))
                    coded_parts.append(((1.0 - before) * (FULL / REACH) + 0.5).astype(jnp.int32))
                    row = rank * 4 + odd
                    place = pl.ds(SUB * half, SUB)
                    out_ref[place, tile, row, :] = coded_parts[0] | lax.shift_left(coded_parts[1], 16)
                    out_ref[place, tile, row + 2, :] = coded_parts[2] | lax.shift_left(coded_parts[3], 16)
        return 0

    lax.fori_loop(0, tiles, one_tile, 0)


def compose_kernel(source_ref, received_ref, out_ref, ordered, *, depths, per_tile):
    groups = per_tile // SUB

    def one_depth(depth, state):
        for foot in range(per_tile):
            source = source_ref[depth, foot]
            block = received_ref[pl.ds(pl.multiple_of(jnp.maximum(source, 0) * 4, 4), 4), :]
            ordered[depth, 4 * foot : 4 * foot + 4, :] = jnp.where(source >= 0, block, 0)
        new = []
        for group in range(groups):
            for odd in range(2):
                red, green, blue, clear = state[group * 2 + odd]
                first = ordered[depth, pl.ds(32 * group + odd, SUB, stride=4), :]
                second = ordered[depth, pl.ds(32 * group + 2 + odd, SUB, stride=4), :]

                def squared(x):
                    x = x.astype(jnp.float32)
                    return x * x

                scaled = clear * (REACH / (FULL * FULL))
                red = red + scaled * squared(first & 0xFFFF)
                green = green + scaled * squared(lax.shift_right_logical(first, 16))
                blue = blue + scaled * squared(second & 0xFFFF)
                clear = clear - clear * (lax.shift_right_logical(second, 16).astype(jnp.float32) * (REACH / FULL))
                new.append((red, green, blue, clear))
        return new

    none = jnp.zeros((SUB, LANES), jnp.float32)
    state = [(none, none, none, none + 1.0) for _ in range(groups * 2)]
    state = lax.fori_loop(0, depths, one_depth, state)
    for group in range(groups):
        for odd in range(2):
            for c in range(4):
                out_ref[c, SUB * group : SUB * group + SUB, LANES * odd : LANES * odd + LANES] = state[group * 2 + odd][c]


def per_device(pool, page_table, tf_bins, palette):
    tiles = lax.axis_size("tile")
    depths = lax.axis_size("depth")
    tile = lax.axis_index("tile")
    page_count, cells, pixels = pool.shape[1], pool.shape[3], pool.shape[4]
    per_tile = page_table.shape[1] // tiles
    columns = pixels // LANES

    rows = page_table[:, :]
    gathered = lax.all_gather(rows, "depth", axis=0, tiled=True)

    bricks = pool[0].reshape(page_count, 4, cells, columns, LANES).transpose(0, 1, 3, 2, 4)
    bricks = bricks.reshape(page_count, 4, columns * cells, LANES)
    messages = pl.pallas_call(
        functools.partial(render_kernel, tiles=tiles, per_tile=per_tile, page_count=page_count),
        out_shape=jax.ShapeDtypeStruct((depths, tiles, SUB, LANES), jnp.int32),
        in_specs=[
            pl.BlockSpec(memory_space=pltpu.SMEM),
            pl.BlockSpec(memory_space=pltpu.VMEM),
            pl.BlockSpec(memory_space=pltpu.VMEM),
            pl.BlockSpec(memory_space=pltpu.HBM),
        ],
        out_specs=pl.BlockSpec(memory_space=pltpu.VMEM),
        scratch_shapes=[
            pltpu.VMEM((SLOTS, CAP, 4, columns * cells, LANES), jnp.bfloat16),
            pltpu.VMEM((CAP, 4, columns * cells, LANES), jnp.float32),
            pltpu.VMEM((SUB, LANES), jnp.float32),
            pltpu.SemaphoreType.DMA((SLOTS, CAP)),
        ],
        compiler_params=pltpu.CompilerParams(vmem_limit_bytes=60 * 1024 * 1024),
        name="render",
    )(page_table, tf_bins.reshape(2, LANES), palette, bricks)

    received = lax.all_to_all(
        messages.reshape(depths * tiles, SUB, LANES), ("depth", "tile"), split_axis=0, concat_axis=0, tiled=True
    )

    own = lax.dynamic_slice_in_dim(gathered, tile * per_tile, per_tile, 1)
    holder = jnp.where(own >= 0, own // page_count, -1)
    foot = jnp.arange(per_tile)
    earlier = (holder[:, :, None] == holder[:, None, :]) & (foot[None, :, None] > foot[None, None, :])
    rank = jnp.any(earlier, axis=2).astype(jnp.int32)
    source = (jnp.arange(depths)[:, None] * tiles + holder) * CAP + rank
    source = jnp.where(own >= 0, source, -1)

    return pl.pallas_call(
        functools.partial(compose_kernel, depths=depths, per_tile=per_tile),
        out_shape=jax.ShapeDtypeStruct((4, per_tile, pixels // depths), jnp.float32),
        in_specs=[pl.BlockSpec(memory_space=pltpu.SMEM), pl.BlockSpec(memory_space=pltpu.VMEM)],
        out_specs=pl.BlockSpec(memory_space=pltpu.VMEM),
        scratch_shapes=[pltpu.VMEM((depths, 4 * per_tile, LANES), jnp.int32)],
        compiler_params=pltpu.CompilerParams(vmem_limit_bytes=24 * 1024 * 1024),
        name="compose",
    )(source, received.reshape(depths * tiles * SUB, LANES))


def solution(mesh):
    in_specs = (P("depth", "tile", None, None, None), P("depth", None), P(), P())
    out_specs = P(None, "tile", "depth")
    return jax.shard_map(per_device, mesh=mesh, in_specs=in_specs, out_specs=out_specs, check_vma=False)
```

time: 1090 us -> 67.3 us (0.06)
  matrix products: 559 us -> 0 us
  waiting for transfers between devices: 439 us -> 11.8 us
  other arithmetic: 48.3 us -> 0.58 us
  blocking collectives: 0 us -> 20 us
  local copies, waits for them, and re-layouts: 19.3 us -> 0.09 us
  Pallas kernels: 0 us -> 18.9 us
  between operations: 13.5 us -> 0.05 us
    dot_general x35 -> x0, matrix products: 559 us -> none  [the longest x32 549 us: one_brick(): jnp.dot(colour_table, hats, precision=lax.Precision.HIGHEST)]
    all_gather x1 -> x0, waiting for transfers between devices: 202 us -> none  [carried_in(): gathered = lax.all_gather(part, axis)]
    psum x1 -> x0, waiting for transfers between devices: 144 us -> none  [from_root(): return lax.psum(block, axis)]
    all_to_all x1, waiting for transfers between devices: 93.2 us -> 11.8 us  [per_device(): lax.all_to_all(messages.reshape(depths * tiles, SUB, LANES), ('depth', 't...]
    convert_element_type x32 -> x0, other arithmetic: 29.7 us -> none  [one_brick(): values = single.astype(jnp.float32)]
    all_gather x0 -> x1, blocking collectives: none -> 20 us  [per_device(): gathered = lax.all_gather(rows, 'depth', axis=0, tiled=True)]
    pallas_call x0 -> x2, Pallas kernels: none -> 18.9 us  [the longest x1 16 us: per_device(): pl.pallas_call(functools.partial(render_kernel, tiles=tiles, per_tile=per...]
  transfers between devices with their start and end apart: 3 -> 1, of which waited for: 3 -> 1; matrix products, arithmetic and copies ran while one was open for 0% -> 1% of each run, Pallas kernels for 0% -> 0%
where the time goes in v1:
time: 67.3 us; the launch traced here: 67.1 us
  blocking collectives  20 us (30%)
  Pallas kernels  18.9 us (28%)
  starting transfers between devices  15.7 us (23%)
  waiting for transfers between devices  11.8 us (18%)
    all_gather x1, blocking collectives, per_device(): gathered = lax.all_gather(rows, 'depth', axis=0, tiled=True)  20 us
    pallas_call x1, Pallas kernels, per_device(): pl.pallas_call(functools.partial(render_kernel, tiles=tiles, per_tile=per...  16 us
    all_to_all x1, starting transfers between devices, per_device(): lax.all_to_all(messages.reshape(depths * tiles, SUB, LANES), ('depth', 't...  15.7 us
    all_to_all x1, waiting for transfers between devices, per_device(): lax.all_to_all(messages.reshape(depths * tiles, SUB, LANES), ('depth', 't...  11.8 us
    pallas_call x1, Pallas kernels, per_device(): pl.pallas_call(functools.partial(compose_kernel, depths=depths, per_tile=...  2.87 us
  transfers between devices with their start and end apart: 1, of which 1 were waited for; matrix products, arithmetic and copies ran while one was open for 1% of the time, Pallas kernels for 0%

profile of v1, /device:TPU:1, one launch (start us, length us, event | category | flops | bytes accessed | tf_op | source)
XLA Modules:
  0.0 67.1 jit_solution(7464902280922924902)
XLA Ops:
  0.0 0.0 copy-start
  0.0 16.0 %render.1 = s32[16,16,8,128]{3,2,1,0:T(8,128)} custom-call(s32[1,512]{1,0:T(1,128)} %table_ref.1, s32[2,128]{1,0:T(2,128)} %bitcast.31, f32[4,16]{1,0:T(4,128)} %palette_ref.1, bf16[48,4,128,128]{3,2,1,0:T(8,128)(2,1)} %bitcast.26), custom_call_target="tpu_custom_call" | custom-call | tf_op jit(solution)/shard_map/render/pallas_call | solution.py:182
  16.0 15.7 %all-to-all-start = ((s32[256,8,128]{2,1,0:T(8,128)}), s32[256,8,128]{2,1,0:T(8,128)S(1)}, u32[]{:S(2)}, u32[]{:S(2)}) async-start(s32[256,8,128]{2,1,0:T(8,128)} %bitcast.27), calls=%async_computation | async-start | bytes 2097152 | tf_op jit(solution)/shard_map/all_to_all | solution.py:202
  31.7 0.0 copy-done
  31.7 20.0 %all-gather = s32[16,1,512]{2,1,0:T(1,128)S(1)} all-gather(s32[1,1,512]{2,1,0:T(1,128)S(1)} %bitcast.30), channel_id=1, replica_groups=mesh['depth'=16,'tile'=16] {'depth'}, dimensions={0}, use_global_device_ids=true | all-gather | bytes 34816 | tf_op jit(solution)/shard_map/all_gather | solution.py:178
  51.8 0.1 constant_dynamic-slice_fusion
  51.9 0.5 and_reduce_fusion
  52.3 0.1 add_select_fusion.1.source_ref
  52.4 11.8 %all-to-all-done = s32[256,8,128]{2,1,0:T(8,128)S(1)} async-done(((s32[256,8,128]{2,1,0:T(8,128)}), s32[256,8,128]{2,1,0:T(8,128)S(1)}, u32[]{:S(2)}, u32[]{:S(2)}) %all-to-all-start) | async-done | bytes 1048608 | tf_op jit(solution)/shard_map/all_to_all | solution.py:202
  64.2 2.9 %compose.1 = f32[4,32,256]{2,1,0:T(8,128)} custom-call(s32[16,32]{1,0:T(8,128)S(1)} %add_select_fusion.1.source_ref, s32[2048,128]{1,0:T(8,128)S(1)} %bitcast.25), custom_call_target="tpu_custom_call" | custom-call | tf_op jit(solution)/shard_map/compose/pallas_call | solution.py:214
  (3 shorter events, 0.0 us)
Async XLA Ops:
  0.0 31.7 %copy-start = (s32[1,512]{1,0:T(1,128)S(1)}, s32[1,512]{1,0:T(1,128)}, u32[]{:S(2)}) copy-start(s32[1,512]{1,0:T(1,128)} %table_ref.1) | copy-start | bytes 6148
  16.0 48.2 %all-to-all-start = ((s32[256,8,128]{2,1,0:T(8,128)}), s32[256,8,128]{2,1,0:T(8,128)S(1)}, u32[]{:S(2)}, u32[]{:S(2)}) async-start(s32[256,8,128]{2,1,0:T(8,128)} %bitcast.27), calls=%async_computation | async-start | bytes 2097152 | tf_op jit(solution)/shard_map/all_to_all | solution.py:202

commit v2 on v1

v2 whole, which is shorter than its diff:
```python
import functools

import jax
import jax.numpy as jnp
from jax import lax
from jax.experimental import pallas as pl
from jax.experimental.pallas import tpu as pltpu
from jax.sharding import PartitionSpec as P

BINS = 256
LANES = 128
SUB = 8
CAP = 2
FOOT = 32
SHARE = 256
LIGHT_X = 0.48
LIGHT_Y = 0.6
LIGHT_Z = 0.64
LOG2E = 1.4426950408889634
FULL = 65535.0
HALF = 32768
REACH = 0.2213
KEY = 64
SHIFT = 16
STEP = 4


def render_kernel(
    table_ref, bins_ref, palette_ref, pool_ref, out_ref, pages, cells32, wide, staged, found_scalar, sems, out_sems, *, tiles, page_count
):
    local = table_ref[...] - lax.axis_index("tile") * page_count
    here = (local >= 0) & (local < page_count)
    key = (lax.broadcasted_iota(jnp.int32, local.shape, 1) & (FOOT - 1)) * KEY + local
    least = jnp.where(here, key, FOOT * KEY)
    largest = jnp.where(here, key, -1)
    step = 1
    while step < FOOT:
        least = jnp.minimum(least, pltpu.roll(least, step, 1))
        largest = jnp.maximum(largest, pltpu.roll(largest, step, 1))
        step *= 2
    one = jnp.where(largest >= 0, KEY | (least & (KEY - 1)), 0)
    two = jnp.where(largest > least, KEY | (largest & (KEY - 1)), 0)
    both_found = one | lax.shift_left(two, SHIFT)
    picked = [both_found[tile // 4, (tile % 4) * FOOT + FOOT - 1] for tile in range(tiles)]

    def fetch(tile, rank, page):
        return pltpu.make_async_copy(pool_ref.at[page], pages.at[tile, rank], sems.at[tile, rank])

    def begin(tile):
        both = picked[tile]
        found_scalar[tile] = both
        fetch(tile, 0, both & (KEY - 1)).start()
        fetch(tile, 1, lax.shift_right_logical(both, SHIFT) & (KEY - 1)).start()

    for tile in range(tiles):
        begin(tile)

    def gather(table, index):
        return jnp.take_along_axis(table, index, axis=1, mode="promise_in_bounds")

    wide[...] = jnp.zeros_like(wide)
    wide[0:4, 0:16] = palette_ref[...]
    palette = wide[...]
    low_bins = jnp.broadcast_to(bins_ref[0:1, :], (SUB, LANES))
    high_bins = jnp.broadcast_to(bins_ref[1:2, :], (SUB, LANES))
    lane = lax.broadcasted_iota(jnp.int32, (SUB, LANES), 1)
    zero = jnp.zeros((SUB, LANES), jnp.int32)
    following = (lane + 1) & (LANES - 1)
    high_next = gather(high_bins, following)
    low_next = jnp.where(lane == LANES - 1, gather(high_bins, zero), gather(low_bins, following))

    def coded(bins, next_bins):
        value = gather(palette, bins) * FULL
        whole = (value + 0.5).astype(jnp.int32)
        change = (gather(palette, next_bins) * FULL - value) * 0.5 - whole.astype(jnp.float32) * (1.0 / 65536.0)
        step = (change + (HALF + 0.5)).astype(jnp.int32) - HALF
        return lax.shift_left(step, 16) | whole

    low_table = coded(low_bins, low_next)
    high_table = coded(high_bins, high_next)
    tables = []
    for channel in range(4):
        tables.append(
            tuple(jnp.broadcast_to(t[channel : channel + 1, :], (SUB, LANES)) for t in (low_table, high_table))
        )

    def send(turn):
        return pltpu.make_async_copy(staged.at[turn], out_ref.at[:, pl.ds(turn * STEP, STEP)], out_sems.at[turn])

    def some_tiles(turn, _):
        first = turn * STEP
        for part in range(CAP * STEP):
            fetch(first + part // CAP, part % CAP, 0).wait()
        for part in range(CAP * STEP):
            tile, rank = first + part // CAP, part % CAP
            filled = (found_scalar[tile] & (KEY << (SHIFT * rank))) != 0
            for field in range(4):
                cells32[part, field] = pages[tile, rank, field].astype(jnp.float32)
            for half in range(2):
                for odd in range(2):
                    colour = [None] * 3
                    through = None
                    before = None
                    for cell in range(4):
                        rows = pl.ds(64 * half + 4 * odd + cell, SUB, stride=8)
                        scalar, normal_x, normal_y, normal_z = (cells32[part, field, rows, :] for field in range(4))
                        scaled = scalar * (BINS - 1.0)
                        index = scaled.astype(jnp.int32)
                        up = (scaled - index.astype(jnp.float32)) * (1.0 / HALF)
                        upper_half = index >= LANES
                        lane_index = index & (LANES - 1)
                        rgba = []
                        for low, high in tables:
                            both = jnp.where(upper_half, gather(high, lane_index), gather(low, lane_index))
                            rgba.append((both & 0xFFFF).astype(jnp.float32) + both.astype(jnp.float32) * up)
                        facing = (
                            normal_x * (2 * LIGHT_X)
                            + normal_y * (2 * LIGHT_Y)
                            + normal_z * (2 * LIGHT_Z)
                            - (LIGHT_X + LIGHT_Y + LIGHT_Z)
                        )
                        shading = 1.0 + jnp.tanh(facing)
                        optical = rgba[3] * (-LOG2E / (16.0 * FULL))
                        through = optical if cell == 0 else through + optical
                        after = jnp.exp2(through)
                        weight = shading * ((1.0 if cell == 0 else before) - after)
                        before = after
                        for c in range(3):
                            term = rgba[c] * weight
                            colour[c] = term if cell == 0 else colour[c] + term
                    coded_parts = []
                    for c in range(3):
                        square = colour[c] * (0.5 * FULL / REACH)
                        root = square * lax.rsqrt(jnp.maximum(square, 1e-20))
                        coded_parts.append((root + 0.5).astype(jnp.int32))
                    coded_parts.append(((1.0 - before) * (FULL / REACH) + 0.5).astype(jnp.int32))
                    row = rank * 4 + odd
                    words = (
                        coded_parts[0] | lax.shift_left(coded_parts[1], 16),
                        coded_parts[2] | lax.shift_left(coded_parts[3], 16),
                    )
                    place = pl.ds(SUB * half, SUB)
                    for word in range(2):
                        staged[turn, place, part // CAP, row + 2 * word, :] = jnp.where(filled, words[word], 0)
        send(turn).start()
        return 0

    lax.fori_loop(0, tiles // STEP, some_tiles, 0)
    for turn in range(tiles // STEP):
        send(turn).wait()


def compose_kernel(source_ref, received_ref, out_ref, ordered, *, depths, per_tile):
    groups = per_tile // SUB

    def one_depth(depth, state):
        for foot in range(per_tile):
            source = pl.multiple_of(source_ref[depth, foot], 4)
            ordered[depth, 4 * foot : 4 * foot + 4, :] = received_ref[pl.ds(source, 4), :]
        new = []
        for group in range(groups):
            for odd in range(2):
                red, green, blue, clear = state[group * 2 + odd]
                first = ordered[depth, pl.ds(32 * group + odd, SUB, stride=4), :]
                second = ordered[depth, pl.ds(32 * group + 2 + odd, SUB, stride=4), :]

                def squared(x):
                    x = x.astype(jnp.float32)
                    return x * x

                scaled = clear * (REACH / (FULL * FULL))
                red = red + scaled * squared(first & 0xFFFF)
                green = green + scaled * squared(lax.shift_right_logical(first, 16))
                blue = blue + scaled * squared(second & 0xFFFF)
                clear = clear - clear * (lax.shift_right_logical(second, 16).astype(jnp.float32) * (REACH / FULL))
                new.append((red, green, blue, clear))
        return new

    none = jnp.zeros((SUB, LANES), jnp.float32)
    state = [(none, none, none, none + 1.0) for _ in range(groups * 2)]
    state = lax.fori_loop(0, depths, one_depth, state, unroll=4)
    for group in range(groups):
        for odd in range(2):
            for c in range(4):
                out_ref[c, SUB * group : SUB * group + SUB, LANES * odd : LANES * odd + LANES] = state[group * 2 + odd][c]


def render_messages(page_table, tf_bins, palette, pool):
    page_count, cells, pixels = pool.shape[1], pool.shape[3], pool.shape[4]
    depths, tiles = pixels // SHARE, page_table.shape[1] // FOOT
    columns = pixels // LANES
    bricks = pool[0].reshape(page_count, 4, cells, columns, LANES).transpose(0, 1, 3, 2, 4)
    bricks = bricks.reshape(page_count, 4, columns * cells, LANES)
    return pl.pallas_call(
        functools.partial(render_kernel, tiles=tiles, page_count=page_count),
        out_shape=jax.ShapeDtypeStruct((depths, tiles, SUB, LANES), jnp.int32),
        in_specs=[
            pl.BlockSpec(memory_space=pltpu.VMEM),
            pl.BlockSpec(memory_space=pltpu.VMEM),
            pl.BlockSpec(memory_space=pltpu.VMEM),
            pl.BlockSpec(memory_space=pltpu.HBM),
        ],
        out_specs=pl.BlockSpec(memory_space=pltpu.HBM),
        scratch_shapes=[
            pltpu.VMEM((tiles, CAP, 4, columns * cells, LANES), jnp.bfloat16),
            pltpu.VMEM((CAP * STEP, 4, columns * cells, LANES), jnp.float32),
            pltpu.VMEM((SUB, LANES), jnp.float32),
            pltpu.VMEM((tiles // STEP, depths, STEP, SUB, LANES), jnp.int32),
            pltpu.SMEM((tiles,), jnp.int32),
            pltpu.SemaphoreType.DMA((tiles, CAP)),
            pltpu.SemaphoreType.DMA((tiles // STEP,)),
        ],
        compiler_params=pltpu.CompilerParams(vmem_limit_bytes=60 * 1024 * 1024),
        name="render",
    )(page_table.reshape(FOOT * tiles // LANES, LANES), tf_bins.reshape(2, LANES), palette, bricks)


def per_device(pool, page_table, tf_bins, palette):
    tiles = lax.axis_size("tile")
    depths = lax.axis_size("depth")
    tile = lax.axis_index("tile")
    page_count, cells, pixels = pool.shape[1], pool.shape[3], pool.shape[4]
    per_tile = page_table.shape[1] // tiles

    rows = page_table[:, :]
    gathered = lax.all_gather(rows, "depth", axis=0, tiled=True)

    messages = render_messages(page_table, tf_bins, palette, pool)
    received = lax.all_to_all(
        messages.reshape(depths * tiles, SUB, LANES), ("depth", "tile"), split_axis=0, concat_axis=0, tiled=True
    )

    own = lax.dynamic_slice_in_dim(gathered, tile * per_tile, per_tile, 1)
    holder = jnp.where(own >= 0, own // page_count, -1)
    foot = jnp.arange(per_tile)
    earlier = (holder[:, :, None] == holder[:, None, :]) & (foot[None, :, None] > foot[None, None, :])
    rank = jnp.any(earlier, axis=2).astype(jnp.int32)
    source = (jnp.arange(depths)[:, None] * tiles + holder) * CAP + rank
    held = jnp.sum((holder[:, None, :] == jnp.arange(tiles)[None, :, None]).astype(jnp.int32), axis=2)
    last = (jnp.arange(depths)[:, None] * tiles + jnp.arange(tiles)[None, :]) * CAP + CAP - 1
    empty = jnp.max(jnp.where(held < CAP, last, 0), axis=1)
    source = jnp.where(own >= 0, source, empty[:, None]) * 4

    return pl.pallas_call(
        functools.partial(compose_kernel, depths=depths, per_tile=per_tile),
        out_shape=jax.ShapeDtypeStruct((4, per_tile, pixels // depths), jnp.float32),
        in_specs=[pl.BlockSpec(memory_space=pltpu.SMEM), pl.BlockSpec(memory_space=pltpu.VMEM)],
        out_specs=pl.BlockSpec(memory_space=pltpu.VMEM),
        scratch_shapes=[pltpu.VMEM((depths, 4 * per_tile, LANES), jnp.int32)],
        compiler_params=pltpu.CompilerParams(vmem_limit_bytes=24 * 1024 * 1024),
        name="compose",
    )(source, received.reshape(depths * tiles * SUB, LANES))


def solution(mesh):
    in_specs = (P("depth", "tile", None, None, None), P("depth", None), P(), P())
    out_specs = P(None, "tile", "depth")
    return jax.shard_map(per_device, mesh=mesh, in_specs=in_specs, out_specs=out_specs, check_vma=False)
```

time: 67.3 us -> 60.6 us (0.900)
  Pallas kernels: 18.9 us -> 12.6 us
    pallas_call x1, Pallas kernels: 16 us -> 10.8 us  [render_messages(): pl.pallas_call(functools.partial(render_kernel, tiles=tiles, page_count=p...]
    pallas_call x1, Pallas kernels: 2.87 us -> 1.86 us  [per_device(): pl.pallas_call(functools.partial(compose_kernel, depths=depths, per_tile=...]
  transfers between devices with their start and end apart: 1 -> 1, of which waited for: 1 -> 1; matrix products, arithmetic and copies ran while one was open for 1% -> 2% of each run, Pallas kernels for 0% -> 0%
where the time goes in v2:
time: 60.6 us
  blocking collectives  20 us (33%)
  starting transfers between devices  15.4 us (25%)
  Pallas kernels  12.6 us (21%)
  waiting for transfers between devices  11.2 us (18%)
  other arithmetic  1.11 us (2%)
    all_gather x1, blocking collectives, per_device(): gathered = lax.all_gather(rows, 'depth', axis=0, tiled=True)  20 us
    all_to_all x1, starting transfers between devices, per_device(): lax.all_to_all(messages.reshape(depths * tiles, SUB, LANES), ('depth', 't...  15.4 us
    all_to_all x1, waiting for transfers between devices, per_device(): lax.all_to_all(messages.reshape(depths * tiles, SUB, LANES), ('depth', 't...  11.2 us
    pallas_call x1, Pallas kernels, render_messages(): pl.pallas_call(functools.partial(render_kernel, tiles=tiles, page_count=p...  10.8 us
    pallas_call x1, Pallas kernels, per_device(): pl.pallas_call(functools.partial(compose_kernel, depths=depths, per_tile=...  1.86 us
  transfers between devices with their start and end apart: 1, of which 1 were waited for; matrix products, arithmetic and copies ran while one was open for 2% of the time, Pallas kernels for 0%

profile of v2, /device:TPU:1, one launch (start us, length us, event | category | flops | bytes accessed | tf_op | source)
XLA Modules:
  0.0 60.6 jit_solution(15937172249994749511)
XLA Ops:
  0.0 0.0 copy-start
  0.0 10.8 %render.1 = s32[16,16,8,128]{3,2,1,0:T(8,128)} custom-call(s32[4,128]{1,0:T(4,128)} %bitcast.31, s32[2,128]{1,0:T(2,128)} %bitcast.33, f32[4,16]{1,0:T(4,128)} %palette_ref.1, bf16[48,4,128,128]{3,2,1,0:T(8,128)(2,1)} %bitcast.27), custom_call_target="tpu_custom_call" | custom-call | tf_op jit(solution)/shard_map/render/pallas_call | solution.py:194
  10.8 15.4 %all-to-all-start = ((s32[256,8,128]{2,1,0:T(8,128)}), s32[256,8,128]{2,1,0:T(8,128)S(1)}, u32[]{:S(2)}, u32[]{:S(2)}) async-start(s32[256,8,128]{2,1,0:T(8,128)} %bitcast.28), calls=%async_computation | async-start | bytes 2097152 | tf_op jit(solution)/shard_map/all_to_all | solution.py:229
  26.2 0.0 copy-done
  26.2 20.0 %all-gather = s32[16,1,512]{2,1,0:T(1,128)S(1)} all-gather(s32[1,1,512]{2,1,0:T(1,128)S(1)} %bitcast.32), channel_id=1, replica_groups=mesh['depth'=16,'tile'=16] {'depth'}, dimensions={0}, use_global_device_ids=true | all-gather | bytes 34816 | tf_op jit(solution)/shard_map/all_gather | solution.py:226
  46.3 0.1 constant_dynamic-slice_fusion
  46.4 0.3 convert_reduce_fusion
  46.7 0.2 select_reduce_fusion
  46.9 0.5 and_reduce_fusion
  47.4 0.1 select_multiply_fusion.source_ref
  47.5 11.2 %all-to-all-done = s32[256,8,128]{2,1,0:T(8,128)S(1)} async-done(((s32[256,8,128]{2,1,0:T(8,128)}), s32[256,8,128]{2,1,0:T(8,128)S(1)}, u32[]{:S(2)}, u32[]{:S(2)}) %all-to-all-start) | async-done | bytes 1048608 | tf_op jit(solution)/shard_map/all_to_all | solution.py:229
  58.7 1.9 %compose.1 = f32[4,32,256]{2,1,0:T(8,128)} custom-call(s32[16,32]{1,0:T(8,128)S(1)} %select_multiply_fusion.source_ref, s32[2048,128]{1,0:T(8,128)S(1)} %bitcast.26), custom_call_target="tpu_custom_call" | custom-call | tf_op jit(solution)/shard_map/compose/pallas_call | solution.py:244
  (3 shorter events, 0.0 us)
Async XLA Ops:
  0.0 26.2 %copy-start = (s32[1,512]{1,0:T(1,128)S(1)}, s32[1,512]{1,0:T(1,128)}, u32[]{:S(2)}) copy-start(s32[1,512]{1,0:T(1,128)} %param.5) | copy-start | bytes 6148
  10.8 47.9 %all-to-all-start = ((s32[256,8,128]{2,1,0:T(8,128)}), s32[256,8,128]{2,1,0:T(8,128)S(1)}, u32[]{:S(2)}, u32[]{:S(2)}) async-start(s32[256,8,128]{2,1,0:T(8,128)} %bitcast.28), calls=%async_computation | async-start | bytes 2097152 | tf_op jit(solution)/shard_map/all_to_all | solution.py:229

commit v3 on v2

--- a/solution.py
+++ b/solution.py
@@ -85,7 +85,7 @@
         )
 
     def send(turn):
-        return pltpu.make_async_copy(staged.at[turn], out_ref.at[:, pl.ds(turn * STEP, STEP)], out_sems.at[turn])
+        return pltpu.make_async_copy(staged.at[turn], out_ref.at[pl.ds(turn * STEP, STEP)], out_sems.at[turn])
 
     def some_tiles(turn, _):
         first = turn * STEP
@@ -141,7 +141,7 @@
                     )
                     place = pl.ds(SUB * half, SUB)
                     for word in range(2):
-                        staged[turn, place, part // CAP, row + 2 * word, :] = jnp.where(filled, words[word], 0)
+                        staged[turn, part // CAP, place, row + 2 * word, :] = jnp.where(filled, words[word], 0)
         send(turn).start()
         return 0
 
@@ -178,7 +178,7 @@
 
     none = jnp.zeros((SUB, LANES), jnp.float32)
     state = [(none, none, none, none + 1.0) for _ in range(groups * 2)]
-    state = lax.fori_loop(0, depths, one_depth, state, unroll=4)
+    state = lax.fori_loop(0, depths, one_depth, state, unroll=16)
     for group in range(groups):
         for odd in range(2):
             for c in range(4):
@@ -193,7 +193,7 @@
     bricks = bricks.reshape(page_count, 4, columns * cells, LANES)
     return pl.pallas_call(
         functools.partial(render_kernel, tiles=tiles, page_count=page_count),
-        out_shape=jax.ShapeDtypeStruct((depths, tiles, SUB, LANES), jnp.int32),
+        out_shape=jax.ShapeDtypeStruct((tiles, depths, SUB, LANES), jnp.int32),
         in_specs=[
             pl.BlockSpec(memory_space=pltpu.VMEM),
             pl.BlockSpec(memory_space=pltpu.VMEM),
@@ -205,7 +205,7 @@
             pltpu.VMEM((tiles, CAP, 4, columns * cells, LANES), jnp.bfloat16),
             pltpu.VMEM((CAP * STEP, 4, columns * cells, LANES), jnp.float32),
             pltpu.VMEM((SUB, LANES), jnp.float32),
-            pltpu.VMEM((tiles // STEP, depths, STEP, SUB, LANES), jnp.int32),
+            pltpu.VMEM((tiles // STEP, STEP, depths, SUB, LANES), jnp.int32),
             pltpu.SMEM((tiles,), jnp.int32),
             pltpu.SemaphoreType.DMA((tiles, CAP)),
             pltpu.SemaphoreType.DMA((tiles // STEP,)),
@@ -227,7 +227,7 @@
 
     messages = render_messages(page_table, tf_bins, palette, pool)
     received = lax.all_to_all(
-        messages.reshape(depths * tiles, SUB, LANES), ("depth", "tile"), split_axis=0, concat_axis=0, tiled=True
+        messages.reshape(tiles * depths, SUB, LANES), ("tile", "depth"), split_axis=0, concat_axis=0, tiled=True
     )
 
     own = lax.dynamic_slice_in_dim(gathered, tile * per_tile, per_tile, 1)
@@ -235,9 +235,9 @@
     foot = jnp.arange(per_tile)
     earlier = (holder[:, :, None] == holder[:, None, :]) & (foot[None, :, None] > foot[None, None, :])
     rank = jnp.any(earlier, axis=2).astype(jnp.int32)
-    source = (jnp.arange(depths)[:, None] * tiles + holder) * CAP + rank
+    source = (holder * depths + jnp.arange(depths)[:, None]) * CAP + rank
     held = jnp.sum((holder[:, None, :] == jnp.arange(tiles)[None, :, None]).astype(jnp.int32), axis=2)
-    last = (jnp.arange(depths)[:, None] * tiles + jnp.arange(tiles)[None, :]) * CAP + CAP - 1
+    last = (jnp.arange(tiles)[None, :] * depths + jnp.arange(depths)[:, None]) * CAP + CAP - 1
     empty = jnp.max(jnp.where(held < CAP, last, 0), axis=1)
     source = jnp.where(own >= 0, source, empty[:, None]) * 4
 

time: 60.6 us -> 58.2 us (0.960)
  waiting for transfers between devices: 11.2 us -> 9.08 us
    all_to_all x1, waiting for transfers between devices: 11.2 us -> 9.08 us  [per_device(): lax.all_to_all(messages.reshape(tiles * depths, SUB, LANES), ('tile', 'de...]
where the time goes in v3:
time: 58.2 us; the launch traced here: 58 us
  blocking collectives  20.1 us (35%)
  starting transfers between devices  15.4 us (26%)
  Pallas kernels  12.2 us (21%)
  waiting for transfers between devices  9.08 us (16%)
  other arithmetic  1.05 us (2%)
    all_gather x1, blocking collectives, per_device(): gathered = lax.all_gather(rows, 'depth', axis=0, tiled=True)  20.1 us
    all_to_all x1, starting transfers between devices, per_device(): lax.all_to_all(messages.reshape(tiles * depths, SUB, LANES), ('tile', 'de...  15.4 us
    pallas_call x1, Pallas kernels, render_messages(): pl.pallas_call(functools.partial(render_kernel, tiles=tiles, page_count=p...  10.5 us
    all_to_all x1, waiting for transfers between devices, per_device(): lax.all_to_all(messages.reshape(tiles * depths, SUB, LANES), ('tile', 'de...  9.08 us
    pallas_call x1, Pallas kernels, per_device(): pl.pallas_call(functools.partial(compose_kernel, depths=depths, per_tile=...  1.73 us
  transfers between devices with their start and end apart: 1, of which 1 were waited for; matrix products, arithmetic and copies ran while one was open for 2% of the time, Pallas kernels for 0%

profile of v3, /device:TPU:1, one launch (start us, length us, event | category | flops | bytes accessed | tf_op | source)
XLA Modules:
  0.0 58.0 jit_solution(10728698234863482224)
XLA Ops:
  0.0 0.0 copy-start
  0.0 10.5 %render.1 = s32[16,16,8,128]{3,2,1,0:T(8,128)} custom-call(s32[4,128]{1,0:T(4,128)} %bitcast.31, s32[2,128]{1,0:T(2,128)} %bitcast.33, f32[4,16]{1,0:T(4,128)} %palette_ref.1, bf16[48,4,128,128]{3,2,1,0:T(8,128)(2,1)} %bitcast.27), custom_call_target="tpu_custom_call" | custom-call | tf_op jit(solution)/shard_map/render/pallas_call | solution.py:194
  10.5 15.4 %all-to-all-start = ((s32[256,8,128]{2,1,0:T(8,128)}), s32[256,8,128]{2,1,0:T(8,128)S(1)}, u32[]{:S(2)}, u32[]{:S(2)}) async-start(s32[256,8,128]{2,1,0:T(8,128)} %bitcast.28), calls=%async_computation | async-start | bytes 2097152 | tf_op jit(solution)/shard_map/all_to_all | solution.py:229
  25.9 0.0 copy-done
  25.9 20.1 %all-gather = s32[16,1,512]{2,1,0:T(1,128)S(1)} all-gather(s32[1,1,512]{2,1,0:T(1,128)S(1)} %bitcast.32), channel_id=1, replica_groups=mesh['depth'=16,'tile'=16] {'depth'}, dimensions={0}, use_global_device_ids=true | all-gather | bytes 34816 | tf_op jit(solution)/shard_map/all_gather | solution.py:226
  46.1 0.1 constant_dynamic-slice_fusion
  46.2 0.3 convert_reduce_fusion
  46.5 0.1 select_reduce_fusion
  46.6 0.5 and_reduce_fusion
  47.1 0.1 select_multiply_fusion.source_ref
  47.2 9.1 %all-to-all-done = s32[256,8,128]{2,1,0:T(8,128)S(1)} async-done(((s32[256,8,128]{2,1,0:T(8,128)}), s32[256,8,128]{2,1,0:T(8,128)S(1)}, u32[]{:S(2)}, u32[]{:S(2)}) %all-to-all-start) | async-done | bytes 1048608 | tf_op jit(solution)/shard_map/all_to_all | solution.py:229
  56.3 1.7 %compose.1 = f32[4,32,256]{2,1,0:T(8,128)} custom-call(s32[16,32]{1,0:T(8,128)S(1)} %select_multiply_fusion.source_ref, s32[2048,128]{1,0:T(8,128)S(1)} %bitcast.26), custom_call_target="tpu_custom_call" | custom-call | tf_op jit(solution)/shard_map/compose/pallas_call | solution.py:244
  (3 shorter events, 0.0 us)
Async XLA Ops:
  0.0 25.9 %copy-start = (s32[1,512]{1,0:T(1,128)S(1)}, s32[1,512]{1,0:T(1,128)}, u32[]{:S(2)}) copy-start(s32[1,512]{1,0:T(1,128)} %param.5) | copy-start | bytes 6148
  10.5 45.8 %all-to-all-start = ((s32[256,8,128]{2,1,0:T(8,128)}), s32[256,8,128]{2,1,0:T(8,128)S(1)}, u32[]{:S(2)}, u32[]{:S(2)}) async-start(s32[256,8,128]{2,1,0:T(8,128)} %bitcast.28), calls=%async_computation | async-start | bytes 2097152 | tf_op jit(solution)/shard_map/all_to_all | solution.py:229

commit v4 on v3

--- a/solution.py
+++ b/solution.py
@@ -1,4 +1,5 @@
 import functools
+import math
 
 import jax
 import jax.numpy as jnp
@@ -20,6 +21,8 @@
 FULL = 65535.0
 HALF = 32768
 REACH = 0.2213
+SCALE = 0.5 * FULL / REACH
+SCALE_LOG2 = math.log2(SCALE)
 KEY = 64
 SHIFT = 16
 STEP = 4
@@ -31,13 +34,12 @@
     local = table_ref[...] - lax.axis_index("tile") * page_count
     here = (local >= 0) & (local < page_count)
     key = (lax.broadcasted_iota(jnp.int32, local.shape, 1) & (FOOT - 1)) * KEY + local
-    least = jnp.where(here, key, FOOT * KEY)
-    largest = jnp.where(here, key, -1)
+    ends = jnp.concatenate([jnp.where(here, key, FOOT * KEY), jnp.where(here, -key, 1)], axis=0)
     step = 1
     while step < FOOT:
-        least = jnp.minimum(least, pltpu.roll(least, step, 1))
-        largest = jnp.maximum(largest, pltpu.roll(largest, step, 1))
+        ends = jnp.minimum(ends, pltpu.roll(ends, step, 1))
         step *= 2
+    least, largest = ends[: local.shape[0]], -ends[local.shape[0] :]
     one = jnp.where(largest >= 0, KEY | (least & (KEY - 1)), 0)
     two = jnp.where(largest > least, KEY | (largest & (KEY - 1)), 0)
     both_found = one | lax.shift_left(two, SHIFT)
@@ -64,25 +66,27 @@
     low_bins = jnp.broadcast_to(bins_ref[0:1, :], (SUB, LANES))
     high_bins = jnp.broadcast_to(bins_ref[1:2, :], (SUB, LANES))
     lane = lax.broadcasted_iota(jnp.int32, (SUB, LANES), 1)
-    zero = jnp.zeros((SUB, LANES), jnp.int32)
-    following = (lane + 1) & (LANES - 1)
-    high_next = gather(high_bins, following)
-    low_next = jnp.where(lane == LANES - 1, gather(high_bins, zero), gather(low_bins, following))
-
-    def coded(bins, next_bins):
-        value = gather(palette, bins) * FULL
-        whole = (value + 0.5).astype(jnp.int32)
-        change = (gather(palette, next_bins) * FULL - value) * 0.5 - whole.astype(jnp.float32) * (1.0 / 65536.0)
-        step = (change + (HALF + 0.5)).astype(jnp.int32) - HALF
-        return lax.shift_left(step, 16) | whole
-
-    low_table = coded(low_bins, low_next)
-    high_table = coded(high_bins, high_next)
-    tables = []
-    for channel in range(4):
-        tables.append(
-            tuple(jnp.broadcast_to(t[channel : channel + 1, :], (SUB, LANES)) for t in (low_table, high_table))
-        )
+
+    def colours(bin_index):
+        at = bin_index & (LANES - 1)
+        bins = jnp.where(bin_index < LANES, gather(low_bins, at), gather(high_bins, at))
+        return gather(palette, bins) * FULL
+
+    first, middle, after_it = colours(2 * lane), colours(2 * lane + 1), colours(jnp.minimum(2 * lane + 2, BINS - 1))
+
+    def step_code(change, low_bits):
+        return (change * 0.5 - low_bits.astype(jnp.float32) * (1.0 / 65536.0) + (HALF + 0.5)).astype(jnp.int32) - HALF
+
+    whole = (middle + 0.5).astype(jnp.int32)
+    to_table = lax.shift_left(step_code(middle - first, whole), 16) | whole
+    change = after_it - middle
+    lower = step_code(change, jnp.zeros_like(whole)) & 0xFFFF
+    to_tables = [jnp.broadcast_to(to_table[c : c + 1, :], (SUB, LANES)) for c in range(4)]
+    from_tables = []
+    for c in range(0, 4, 2):
+        low_row = jnp.broadcast_to(lower[c + 1 : c + 2, :], (SUB, LANES))
+        row = jnp.broadcast_to(change[c : c + 1, :], (SUB, LANES))
+        from_tables.append(lax.shift_left(step_code(row, low_row), 16) | low_row)
 
     def send(turn):
         return pltpu.make_async_copy(staged.at[turn], out_ref.at[pl.ds(turn * STEP, STEP)], out_sems.at[turn])
@@ -94,8 +98,15 @@
         for part in range(CAP * STEP):
             tile, rank = first + part // CAP, part % CAP
             filled = (found_scalar[tile] & (KEY << (SHIFT * rank))) != 0
-            for field in range(4):
-                cells32[part, field] = pages[tile, rank, field].astype(jnp.float32)
+            scalar, normal_x, normal_y, normal_z = (pages[tile, rank, field].astype(jnp.float32) for field in range(4))
+            facing = (
+                normal_x * (2 * LIGHT_X)
+                + normal_y * (2 * LIGHT_Y)
+                + normal_z * (2 * LIGHT_Z)
+                - (LIGHT_X + LIGHT_Y + LIGHT_Z)
+            )
+            cells32[part, 0] = scalar * ((BINS - 1.0) / 2)
+            cells32[part, 1] = 1.0 + jnp.tanh(facing)
             for half in range(2):
                 for odd in range(2):
                     colour = [None] * 3
@@ -103,37 +114,35 @@
                     before = None
                     for cell in range(4):
                         rows = pl.ds(64 * half + 4 * odd + cell, SUB, stride=8)
-                        scalar, normal_x, normal_y, normal_z = (cells32[part, field, rows, :] for field in range(4))
-                        scaled = scalar * (BINS - 1.0)
+                        scaled = cells32[part, 0, rows, :]
                         index = scaled.astype(jnp.int32)
-                        up = (scaled - index.astype(jnp.float32)) * (1.0 / HALF)
-                        upper_half = index >= LANES
+                        along = (scaled - index.astype(jnp.float32) - 0.5) * (2.0 / HALF)
+                        to_it, from_it = jnp.minimum(along, 0.0), jnp.maximum(along, 0.0)
                         lane_index = index & (LANES - 1)
+                        tos = [gather(table, lane_index) for table in to_tables]
+                        froms = []
+                        for table in from_tables:
+                            both = gather(table, lane_index)
+                            froms += [both, lax.shift_left(both, 16)]
                         rgba = []
-                        for low, high in tables:
-                            both = jnp.where(upper_half, gather(high, lane_index), gather(low, lane_index))
-                            rgba.append((both & 0xFFFF).astype(jnp.float32) + both.astype(jnp.float32) * up)
-                        facing = (
-                            normal_x * (2 * LIGHT_X)
-                            + normal_y * (2 * LIGHT_Y)
-                            + normal_z * (2 * LIGHT_Z)
-                            - (LIGHT_X + LIGHT_Y + LIGHT_Z)
-                        )
-                        shading = 1.0 + jnp.tanh(facing)
+                        for word, step_on in zip(tos, froms):
+                            value = (word & 0xFFFF).astype(jnp.float32) + word.astype(jnp.float32) * to_it
+                            rgba.append(value + step_on.astype(jnp.float32) * from_it)
+                        shading = cells32[part, 1, rows, :]
                         optical = rgba[3] * (-LOG2E / (16.0 * FULL))
-                        through = optical if cell == 0 else through + optical
+                        through = optical + SCALE_LOG2 if cell == 0 else through + optical
                         after = jnp.exp2(through)
-                        weight = shading * ((1.0 if cell == 0 else before) - after)
+                        weight = shading * ((SCALE if cell == 0 else before) - after)
                         before = after
                         for c in range(3):
                             term = rgba[c] * weight
                             colour[c] = term if cell == 0 else colour[c] + term
                     coded_parts = []
                     for c in range(3):
-                        square = colour[c] * (0.5 * FULL / REACH)
+                        square = colour[c]
                         root = square * lax.rsqrt(jnp.maximum(square, 1e-20))
                         coded_parts.append((root + 0.5).astype(jnp.int32))
-                    coded_parts.append(((1.0 - before) * (FULL / REACH) + 0.5).astype(jnp.int32))
+                    coded_parts.append(((2 * SCALE + 0.5) - before * 2.0).astype(jnp.int32))
                     row = rank * 4 + odd
                     words = (
                         coded_parts[0] | lax.shift_left(coded_parts[1], 16),
@@ -203,7 +212,7 @@
         out_specs=pl.BlockSpec(memory_space=pltpu.HBM),
         scratch_shapes=[
             pltpu.VMEM((tiles, CAP, 4, columns * cells, LANES), jnp.bfloat16),
-            pltpu.VMEM((CAP * STEP, 4, columns * cells, LANES), jnp.float32),
+            pltpu.VMEM((CAP * STEP, 2, columns * cells, LANES), jnp.float32),
             pltpu.VMEM((SUB, LANES), jnp.float32),
             pltpu.VMEM((tiles // STEP, STEP, depths, SUB, LANES), jnp.int32),
             pltpu.SMEM((tiles,), jnp.int32),

time: 58.2 us -> 57.9 us (level)
  no operation moved by 1% of the time
where the time goes in v4:
time: 57.9 us; the launch traced here: 57.7 us
  blocking collectives  20.1 us (35%)
  starting transfers between devices  15.7 us (27%)
  Pallas kernels  11.7 us (20%)
  waiting for transfers between devices  9.08 us (16%)
  other arithmetic  1.05 us (2%)
    all_gather x1, blocking collectives, per_device(): gathered = lax.all_gather(rows, 'depth', axis=0, tiled=True)  20.1 us
    all_to_all x1, starting transfers between devices, per_device(): lax.all_to_all(messages.reshape(tiles * depths, SUB, LANES), ('tile', 'de...  15.7 us
    pallas_call x1, Pallas kernels, render_messages(): pl.pallas_call(functools.partial(render_kernel, tiles=tiles, page_count=p...  9.94 us
    all_to_all x1, waiting for transfers between devices, per_device(): lax.all_to_all(messages.reshape(tiles * depths, SUB, LANES), ('tile', 'de...  9.08 us
    pallas_call x1, Pallas kernels, per_device(): pl.pallas_call(functools.partial(compose_kernel, depths=depths, per_tile=...  1.73 us
  transfers between devices with their start and end apart: 1, of which 1 were waited for; matrix products, arithmetic and copies ran while one was open for 2% of the time, Pallas kernels for 0%

profile of v4, /device:TPU:1, one launch (start us, length us, event | category | flops | bytes accessed | tf_op | source)
XLA Modules:
  0.0 57.7 jit_solution(5150201658292694857)
XLA Ops:
  0.0 0.0 copy-start
  0.0 9.9 %render.1 = s32[16,16,8,128]{3,2,1,0:T(8,128)} custom-call(s32[4,128]{1,0:T(4,128)} %bitcast.31, s32[2,128]{1,0:T(2,128)} %bitcast.33, f32[4,16]{1,0:T(4,128)} %palette_ref.1, bf16[48,4,128,128]{3,2,1,0:T(8,128)(2,1)} %bitcast.27), custom_call_target="tpu_custom_call" | custom-call | tf_op jit(solution)/shard_map/render/pallas_call | solution.py:203
  9.9 15.7 %all-to-all-start = ((s32[256,8,128]{2,1,0:T(8,128)}), s32[256,8,128]{2,1,0:T(8,128)S(1)}, u32[]{:S(2)}, u32[]{:S(2)}) async-start(s32[256,8,128]{2,1,0:T(8,128)} %bitcast.28), calls=%async_computation | async-start | bytes 2097152 | tf_op jit(solution)/shard_map/all_to_all | solution.py:238
  25.6 0.0 copy-done
  25.6 20.1 %all-gather = s32[16,1,512]{2,1,0:T(1,128)S(1)} all-gather(s32[1,1,512]{2,1,0:T(1,128)S(1)} %bitcast.32), channel_id=1, replica_groups=mesh['depth'=16,'tile'=16] {'depth'}, dimensions={0}, use_global_device_ids=true | all-gather | bytes 34816 | tf_op jit(solution)/shard_map/all_gather | solution.py:235
  45.7 0.1 constant_dynamic-slice_fusion
  45.8 0.3 convert_reduce_fusion
  46.2 0.1 select_reduce_fusion
  46.3 0.5 and_reduce_fusion
  46.8 0.1 select_multiply_fusion.source_ref
  46.9 9.1 %all-to-all-done = s32[256,8,128]{2,1,0:T(8,128)S(1)} async-done(((s32[256,8,128]{2,1,0:T(8,128)}), s32[256,8,128]{2,1,0:T(8,128)S(1)}, u32[]{:S(2)}, u32[]{:S(2)}) %all-to-all-start) | async-done | bytes 1048608 | tf_op jit(solution)/shard_map/all_to_all | solution.py:238
  55.9 1.7 %compose.1 = f32[4,32,256]{2,1,0:T(8,128)} custom-call(s32[16,32]{1,0:T(8,128)S(1)} %select_multiply_fusion.source_ref, s32[2048,128]{1,0:T(8,128)S(1)} %bitcast.26), custom_call_target="tpu_custom_call" | custom-call | tf_op jit(solution)/shard_map/compose/pallas_call | solution.py:253
  (3 shorter events, 0.0 us)
Async XLA Ops:
  0.0 25.6 %copy-start = (s32[1,512]{1,0:T(1,128)S(1)}, s32[1,512]{1,0:T(1,128)}, u32[]{:S(2)}) copy-start(s32[1,512]{1,0:T(1,128)} %param.5) | copy-start | bytes 6148
  9.9 46.0 %all-to-all-start = ((s32[256,8,128]{2,1,0:T(8,128)}), s32[256,8,128]{2,1,0:T(8,128)S(1)}, u32[]{:S(2)}, u32[]{:S(2)}) async-start(s32[256,8,128]{2,1,0:T(8,128)} %bitcast.28), calls=%async_computation | async-start | bytes 2097152 | tf_op jit(solution)/shard_map/all_to_all | solution.py:238

commit v5 on v3

--- a/solution.py
+++ b/solution.py
@@ -222,15 +222,14 @@
     page_count, cells, pixels = pool.shape[1], pool.shape[3], pool.shape[4]
     per_tile = page_table.shape[1] // tiles
 
-    rows = page_table[:, :]
-    gathered = lax.all_gather(rows, "depth", axis=0, tiled=True)
+    own_row = lax.dynamic_slice_in_dim(page_table, tile * per_tile, per_tile, 1)
+    own = lax.all_gather(own_row, "depth", axis=0, tiled=True)
 
     messages = render_messages(page_table, tf_bins, palette, pool)
     received = lax.all_to_all(
         messages.reshape(tiles * depths, SUB, LANES), ("tile", "depth"), split_axis=0, concat_axis=0, tiled=True
     )
 
-    own = lax.dynamic_slice_in_dim(gathered, tile * per_tile, per_tile, 1)
     holder = jnp.where(own >= 0, own // page_count, -1)
     foot = jnp.arange(per_tile)
     earlier = (holder[:, :, None] == holder[:, None, :]) & (foot[None, :, None] > foot[None, None, :])

time: 58.2 us -> 58.1 us (level)
  blocking collectives: 20.1 us -> 18 us
  waiting for transfers between devices: 9.08 us -> 10.5 us
  local copies, waits for them, and re-layouts: 0.09 us -> 0.73 us
    all_gather x1, blocking collectives: 20.1 us -> 18 us  [per_device(): own = lax.all_gather(own_row, 'depth', axis=0, tiled=True)]
    all_to_all x1, waiting for transfers between devices: 9.08 us -> 10.5 us  [per_device(): lax.all_to_all(messages.reshape(tiles * depths, SUB, LANES), ('tile', 'de...]
    unnamed x2 -> x1, local copies, waits for them, and re-layouts: 0.01 us -> 0.73 us
  transfers between devices with their start and end apart: 1 -> 1, of which waited for: 1 -> 1; matrix products, arithmetic and copies ran while one was open for 2% -> 3% of each run, Pallas kernels for 0% -> 0%
where the time goes in v5:
time: 58.1 us; the launch traced here: 57.9 us
  blocking collectives  18 us (31%)
  starting transfers between devices  15.7 us (27%)
  Pallas kernels  11.9 us (20%)
  waiting for transfers between devices  10.5 us (18%)
  other arithmetic  1.04 us (2%)
  local copies, waits for them, and re-layouts  0.73 us (1%)
    all_gather x1, blocking collectives, per_device(): own = lax.all_gather(own_row, 'depth', axis=0, tiled=True)  18 us
    all_to_all x1, starting transfers between devices, per_device(): lax.all_to_all(messages.reshape(tiles * depths, SUB, LANES), ('tile', 'de...  15.7 us
    all_to_all x1, waiting for transfers between devices, per_device(): lax.all_to_all(messages.reshape(tiles * depths, SUB, LANES), ('tile', 'de...  10.5 us
    pallas_call x1, Pallas kernels, render_messages(): pl.pallas_call(functools.partial(render_kernel, tiles=tiles, page_count=p...  10.2 us
    pallas_call x1, Pallas kernels, per_device(): pl.pallas_call(functools.partial(compose_kernel, depths=depths, per_tile=...  1.73 us
  transfers between devices with their start and end apart: 1, of which 1 were waited for; matrix products, arithmetic and copies ran while one was open for 3% of the time, Pallas kernels for 0%

profile of v5, /device:TPU:1, one launch (start us, length us, event | category | flops | bytes accessed | tf_op | source)
XLA Modules:
  0.0 57.9 jit_solution(4639588798130356148)
XLA Ops:
  0.0 10.2 %render.1 = s32[16,16,8,128]{3,2,1,0:T(8,128)} custom-call(s32[4,128]{1,0:T(4,128)} %bitcast.32, s32[2,128]{1,0:T(2,128)} %bitcast.33, f32[4,16]{1,0:T(4,128)} %palette_ref.1, bf16[48,4,128,128]{3,2,1,0:T(8,128)(2,1)} %bitcast.28), custom_call_target="tpu_custom_call" | custom-call | tf_op jit(solution)/shard_map/render/pallas_call | solution.py:194
  10.2 15.7 %all-to-all-start = ((s32[256,8,128]{2,1,0:T(8,128)}), s32[256,8,128]{2,1,0:T(8,128)S(1)}, u32[]{:S(2)}, u32[]{:S(2)}) async-start(s32[256,8,128]{2,1,0:T(8,128)} %bitcast.29), calls=%async_computation | async-start | bytes 2097152 | tf_op jit(solution)/shard_map/all_to_all | solution.py:229
  25.9 0.7 %dynamic-slice_bitcast_fusion = s32[1,1,32]{2,1,0:T(1,128)S(1)} fusion(s32[1,512]{1,0:T(1,128)} %param.5, s32[]{:T(128)S(6)} %select_n.20), kind=kLoop, calls=%fused_computation.13 | loop fusion | bytes 260
  26.6 18.0 %all-gather = s32[16,1,32]{2,1,0:T(1,128)S(1)} all-gather(s32[1,1,32]{2,1,0:T(1,128)S(1)} %dynamic-slice_bitcast_fusion), channel_id=1, replica_groups=mesh['depth'=16,'tile'=16] {'depth'}, dimensions={0}, use_global_device_ids=true | all-gather | bytes 2176 | tf_op jit(solution)/shard_map/all_gather | solution.py:226
  44.6 0.3 convert_reduce_fusion
  45.0 0.1 select_reduce_fusion
  45.1 0.5 and_reduce_fusion
  45.6 0.1 select_multiply_fusion.source_ref
  45.7 10.5 %all-to-all-done = s32[256,8,128]{2,1,0:T(8,128)S(1)} async-done(((s32[256,8,128]{2,1,0:T(8,128)}), s32[256,8,128]{2,1,0:T(8,128)S(1)}, u32[]{:S(2)}, u32[]{:S(2)}) %all-to-all-start) | async-done | bytes 1048608 | tf_op jit(solution)/shard_map/all_to_all | solution.py:229
  56.2 1.7 %compose.1 = f32[4,32,256]{2,1,0:T(8,128)} custom-call(s32[16,32]{1,0:T(8,128)S(1)} %select_multiply_fusion.source_ref, s32[2048,128]{1,0:T(8,128)S(1)} %bitcast.27), custom_call_target="tpu_custom_call" | custom-call | tf_op jit(solution)/shard_map/compose/pallas_call | solution.py:243
  (3 shorter events, 0.0 us)
Async XLA Ops:
  10.2 46.0 %all-to-all-start = ((s32[256,8,128]{2,1,0:T(8,128)}), s32[256,8,128]{2,1,0:T(8,128)S(1)}, u32[]{:S(2)}, u32[]{:S(2)}) async-start(s32[256,8,128]{2,1,0:T(8,128)} %bitcast.29), calls=%async_computation | async-start | bytes 2097152 | tf_op jit(solution)/shard_map/all_to_all | solution.py:229

commit v6 on v4

--- a/solution.py
+++ b/solution.py
@@ -231,15 +231,14 @@
     page_count, cells, pixels = pool.shape[1], pool.shape[3], pool.shape[4]
     per_tile = page_table.shape[1] // tiles
 
-    rows = page_table[:, :]
-    gathered = lax.all_gather(rows, "depth", axis=0, tiled=True)
+    own_row = lax.dynamic_slice_in_dim(page_table, tile * per_tile, per_tile, 1)
+    own = lax.all_gather(own_row, "depth", axis=0, tiled=True)
 
     messages = render_messages(page_table, tf_bins, palette, pool)
     received = lax.all_to_all(
         messages.reshape(tiles * depths, SUB, LANES), ("tile", "depth"), split_axis=0, concat_axis=0, tiled=True
     )
 
-    own = lax.dynamic_slice_in_dim(gathered, tile * per_tile, per_tile, 1)
     holder = jnp.where(own >= 0, own // page_count, -1)
     foot = jnp.arange(per_tile)
     earlier = (holder[:, :, None] == holder[:, None, :]) & (foot[None, :, None] > foot[None, None, :])

time: 57.9 us -> 57.9 us (level)
  blocking collectives: 20.1 us -> 18 us
  waiting for transfers between devices: 9.08 us -> 10.5 us
  local copies, waits for them, and re-layouts: 0.09 us -> 0.73 us
    all_gather x1, blocking collectives: 20.1 us -> 18 us  [per_device(): own = lax.all_gather(own_row, 'depth', axis=0, tiled=True)]
    all_to_all x1, waiting for transfers between devices: 9.08 us -> 10.5 us  [per_device(): lax.all_to_all(messages.reshape(tiles * depths, SUB, LANES), ('tile', 'de...]
    unnamed x2 -> x1, local copies, waits for them, and re-layouts: 0.01 us -> 0.73 us
  transfers between devices with their start and end apart: 1 -> 1, of which waited for: 1 -> 1; matrix products, arithmetic and copies ran while one was open for 2% -> 3% of each run, Pallas kernels for 0% -> 0%
where the time goes in v6:
time: 57.9 us; the launch traced here: 57.7 us
  blocking collectives  18 us (31%)
  starting transfers between devices  15.7 us (27%)
  Pallas kernels  11.6 us (20%)
  waiting for transfers between devices  10.5 us (18%)
  other arithmetic  1.04 us (2%)
  local copies, waits for them, and re-layouts  0.73 us (1%)
    all_gather x1, blocking collectives, per_device(): own = lax.all_gather(own_row, 'depth', axis=0, tiled=True)  18 us
    all_to_all x1, starting transfers between devices, per_device(): lax.all_to_all(messages.reshape(tiles * depths, SUB, LANES), ('tile', 'de...  15.7 us
    all_to_all x1, waiting for transfers between devices, per_device(): lax.all_to_all(messages.reshape(tiles * depths, SUB, LANES), ('tile', 'de...  10.5 us
    pallas_call x1, Pallas kernels, render_messages(): pl.pallas_call(functools.partial(render_kernel, tiles=tiles, page_count=p...  9.88 us
    pallas_call x1, Pallas kernels, per_device(): pl.pallas_call(functools.partial(compose_kernel, depths=depths, per_tile=...  1.73 us
  transfers between devices with their start and end apart: 1, of which 1 were waited for; matrix products, arithmetic and copies ran while one was open for 3% of the time, Pallas kernels for 0%

profile of v6, /device:TPU:1, one launch (start us, length us, event | category | flops | bytes accessed | tf_op | source)
XLA Modules:
  0.0 57.7 jit_solution(16201390233297105999)
XLA Ops:
  0.0 9.9 %render.1 = s32[16,16,8,128]{3,2,1,0:T(8,128)} custom-call(s32[4,128]{1,0:T(4,128)} %bitcast.32, s32[2,128]{1,0:T(2,128)} %bitcast.33, f32[4,16]{1,0:T(4,128)} %palette_ref.1, bf16[48,4,128,128]{3,2,1,0:T(8,128)(2,1)} %bitcast.28), custom_call_target="tpu_custom_call" | custom-call | tf_op jit(solution)/shard_map/render/pallas_call | solution.py:203
  9.9 15.7 %all-to-all-start = ((s32[256,8,128]{2,1,0:T(8,128)}), s32[256,8,128]{2,1,0:T(8,128)S(1)}, u32[]{:S(2)}, u32[]{:S(2)}) async-start(s32[256,8,128]{2,1,0:T(8,128)} %bitcast.29), calls=%async_computation | async-start | bytes 2097152 | tf_op jit(solution)/shard_map/all_to_all | solution.py:238
  25.6 0.7 %dynamic-slice_bitcast_fusion = s32[1,1,32]{2,1,0:T(1,128)S(1)} fusion(s32[1,512]{1,0:T(1,128)} %param.5, s32[]{:T(128)S(6)} %select_n.20), kind=kLoop, calls=%fused_computation.13 | loop fusion | bytes 260
  26.4 18.0 %all-gather = s32[16,1,32]{2,1,0:T(1,128)S(1)} all-gather(s32[1,1,32]{2,1,0:T(1,128)S(1)} %dynamic-slice_bitcast_fusion), channel_id=1, replica_groups=mesh['depth'=16,'tile'=16] {'depth'}, dimensions={0}, use_global_device_ids=true | all-gather | bytes 2176 | tf_op jit(solution)/shard_map/all_gather | solution.py:235
  44.4 0.3 convert_reduce_fusion
  44.8 0.1 select_reduce_fusion
  44.9 0.5 and_reduce_fusion
  45.3 0.1 select_multiply_fusion.source_ref
  45.4 10.5 %all-to-all-done = s32[256,8,128]{2,1,0:T(8,128)S(1)} async-done(((s32[256,8,128]{2,1,0:T(8,128)}), s32[256,8,128]{2,1,0:T(8,128)S(1)}, u32[]{:S(2)}, u32[]{:S(2)}) %all-to-all-start) | async-done | bytes 1048608 | tf_op jit(solution)/shard_map/all_to_all | solution.py:238
  56.0 1.7 %compose.1 = f32[4,32,256]{2,1,0:T(8,128)} custom-call(s32[16,32]{1,0:T(8,128)S(1)} %select_multiply_fusion.source_ref, s32[2048,128]{1,0:T(8,128)S(1)} %bitcast.27), custom_call_target="tpu_custom_call" | custom-call | tf_op jit(solution)/shard_map/compose/pallas_call | solution.py:252
  (3 shorter events, 0.0 us)
Async XLA Ops:
  9.9 46.1 %all-to-all-start = ((s32[256,8,128]{2,1,0:T(8,128)}), s32[256,8,128]{2,1,0:T(8,128)S(1)}, u32[]{:S(2)}, u32[]{:S(2)}) async-start(s32[256,8,128]{2,1,0:T(8,128)} %bitcast.29), calls=%async_computation | async-start | bytes 2097152 | tf_op jit(solution)/shard_map/all_to_all | solution.py:238
